TPU v7x, 128 devices: a whole 4x4x4 slice. The times are simulated.
128 devices in a mesh: fsdp: 8 (over x, z_hi), seq: 16 (over z_lo, y, core).
Axes of the slice: x: 4, y: 4, z: 4 (z_hi: 2, z_lo: 2; z = z_hi * 2 + z_lo), core: 2. Of those that a mesh axis runs over, the one named last changes fastest.
Arguments:
- inputs: bfloat16 [8, 6144, 768], P('fsdp', 'seq'), may hold values from -6 to 6
- first_gain: bfloat16 [768], P('fsdp'), may hold values from 0.5 to 1.5
- joint_weight: bfloat16 [768, 2304], P('fsdp'), may hold values from -0.21875 to 0.21875
- merge_weight: bfloat16 [768, 768], P('fsdp'), may hold values from -1.25 to 1.25
- second_gain: bfloat16 [768], P('fsdp'), may hold values from 0.5 to 1.5
- expand_weight: bfloat16 [768, 2304], P('fsdp'), may hold values from -0.21875 to 0.21875
- shrink_weight: bfloat16 [1152, 768], P('fsdp'), may hold values from -0.375 to 0.375
- cotangent: bfloat16 [8, 6144, 768], P('fsdp', 'seq'), may hold values from -6 to 6
Outputs:
- block_out: bfloat16 [8, 6144, 768], P('fsdp', 'seq')
- input_grad: bfloat16 [8, 6144, 768], P('fsdp', 'seq')
- first_grad: float32 [768], P('fsdp')
- joint_grad: float32 [768, 2304], P('fsdp')
- merge_grad: float32 [768, 768], P('fsdp')
- second_grad: float32 [768], P('fsdp')
- expand_grad: float32 [768, 2304], P('fsdp')
- shrink_grad: float32 [1152, 768], P('fsdp')
All inputs are finite; a program needn't handle non-finite values.
Results may differ from a plain program's by a relative error of at most 0.025.
Values may be sent and summed in bfloat16 or wider, within the bound.
No kernel may reach another device: no remote copies, remote signals or barrier semaphores. Data moves between devices by JAX's collectives and lax.ppermute only.
A program may use at most 128 MiB of HBM per device.

v0:
```python
import math

import jax
import jax.numpy as jnp
from jax import lax
from jax.sharding import PartitionSpec as P

D = 768
HEADS = 12
HEAD_DIM = 64
FF = 1152
WINDOW = 128


epsilon = 1e-05


def with_halo(block, sides, width):
    for axis, dim in sides:
        count = lax.axis_size(axis)
        forward = [(i, i + 1) for i in range(count - 1)]
        backward = [(target, source) for source, target in forward]
        low = lax.ppermute(
            lax.slice_in_dim(block, block.shape[dim] - width, None, axis=dim), axis, forward
        )
        high = lax.ppermute(lax.slice_in_dim(block, 0, width, axis=dim), axis, backward)
        block = jnp.concatenate([low, block, high], axis=dim)
    return block


def passed_along(value, axis, steps):
    count = lax.axis_size(axis)
    leading, last = (max(0, -steps), min(count, count - steps))
    return lax.ppermute(value, axis, [(source, source + steps) for source in range(leading, last)])


def outer_sum(left, right):
    return lax.dot_general(
        left, right, (((0,), (0,)), ((), ())), preferred_element_type=jnp.float32
    )


def back_product(left, weight):
    return lax.dot_general(
        left, weight, (((1,), (1,)), ((), ())), preferred_element_type=jnp.float32
    )


def normalize(values):
    centred = values - jnp.mean(values, axis=-1, keepdims=True)
    spread = jnp.mean(centred * centred, axis=-1, keepdims=True)
    inverse = lax.rsqrt(spread + epsilon)
    return (centred * inverse, inverse)


def norm_back(upstream, normed, inverse, gain):
    gain_part = jnp.sum(upstream * normed, axis=0)
    scaled = upstream * gain
    centred = scaled - jnp.mean(scaled, axis=-1, keepdims=True)
    return (
        inverse * (centred - normed * jnp.mean(scaled * normed, axis=-1, keepdims=True)),
        gain_part,
    )


def rotate(values, cosine, sine):
    middle = values.shape[-1] // 2
    former = values[..., :middle]
    latter = values[..., middle:]
    return jnp.concatenate(
        [former * cosine - latter * sine, latter * cosine + former * sine], axis=-1
    )


def unrotate(upstream, cosine, sine):
    middle = upstream.shape[-1] // 2
    former = upstream[..., :middle]
    latter = upstream[..., middle:]
    return jnp.concatenate(
        [former * cosine + latter * sine, latter * cosine - former * sine], axis=-1
    )


def band_windows(extended, tokens, tile_rows):
    tiles = tokens // tile_rows
    lower = extended[:tokens].reshape(tiles, tile_rows, extended.shape[1])
    upper = extended[tile_rows : tokens + tile_rows].reshape(tiles, tile_rows, extended.shape[1])
    return jnp.concatenate([lower, upper], axis=1)


def band_scores(queries, keys_all, offset, seq_length, rim_width):
    scores = jnp.einsum(
        "tqhd,tkhd->thqk", queries, keys_all, preferred_element_type=jnp.float32
    ) * (1.0 / math.sqrt(HEAD_DIM))
    tiles = queries.shape[0]
    row_count = queries.shape[1]
    col_count = keys_all.shape[1]
    shape = (tiles, row_count, col_count)
    query_pos = lax.broadcasted_iota(jnp.int32, shape, 1)
    key_pos = lax.broadcasted_iota(jnp.int32, shape, 2) - rim_width
    tile_base = lax.broadcasted_iota(jnp.int32, shape, 0) * row_count
    global_key = offset + tile_base + key_pos
    allowed = (
        (jnp.abs(query_pos - key_pos) <= rim_width) & (global_key >= 0) & (global_key < seq_length)
    )
    return jnp.where(allowed[:, None], scores, -1e30)


def shards(
    inputs,
    first_gain,
    joint_weight,
    merge_weight,
    second_gain,
    expand_weight,
    shrink_weight,
    cotangent,
):
    tokens = inputs.shape[1]
    rim_width = WINDOW // 2
    tile_rows = 2 * rim_width
    tiles = tokens // tile_rows
    offset = lax.axis_index("seq") * tokens
    seq_length = tokens * lax.axis_size("seq")
    gathered = (
        lax.all_gather(first_gain, "fsdp", axis=0, tiled=True),
        lax.all_gather(joint_weight, "fsdp", axis=0, tiled=True),
        lax.all_gather(merge_weight, "fsdp", axis=0, tiled=True),
        lax.all_gather(second_gain, "fsdp", axis=0, tiled=True),
        lax.all_gather(expand_weight, "fsdp", axis=0, tiled=True),
        lax.all_gather(shrink_weight, "fsdp", axis=0, tiled=True),
    )
    gain_one = gathered[0].astype(jnp.float32)
    joint_w = gathered[1]
    merge_w = gathered[2]
    gain_two = gathered[3].astype(jnp.float32)
    expand_w = gathered[4]
    shrink_w = gathered[5]
    frequencies = jnp.exp(
        jnp.arange(HEAD_DIM // 2, dtype=jnp.float32) * (-2.0 * math.log(10000.0) / HEAD_DIM)
    )
    positions = (offset + lax.iota(jnp.int32, tokens)).astype(jnp.float32)
    angles = positions[:, None] * frequencies[None, :]
    cosine = jnp.cos(angles)[:, None, :]
    sine = jnp.sin(angles)[:, None, :]
    source = inputs[0].astype(jnp.float32)
    normed_one, inverse_one = normalize(source)
    h_first = (normed_one * gain_one).astype(jnp.bfloat16)
    joint = jnp.dot(h_first, joint_w, preferred_element_type=jnp.float32)
    queries = rotate(joint[:, :D].reshape(tokens, HEADS, HEAD_DIM), cosine, sine).astype(
        jnp.bfloat16
    )
    keys_rot = rotate(joint[:, D : 2 * D].reshape(tokens, HEADS, HEAD_DIM), cosine, sine).astype(
        jnp.bfloat16
    )
    values_b = joint[:, 2 * D :].astype(jnp.bfloat16)
    paired = jnp.concatenate([keys_rot.reshape(tokens, D), values_b], axis=1)
    extended = with_halo(paired, (("seq", 0),), rim_width)
    windows = band_windows(extended, tokens, tile_rows)
    col_count = windows.shape[1]
    keys_all = windows[:, :, :D].reshape(tiles, col_count, HEADS, HEAD_DIM)
    values_all = windows[:, :, D:].reshape(tiles, col_count, HEADS, HEAD_DIM)
    queries_t = queries.reshape(tiles, tile_rows, HEADS, HEAD_DIM)
    scores = band_scores(queries_t, keys_all, offset, seq_length, rim_width)
    highest = jnp.max(scores, axis=-1, keepdims=True)
    expo = jnp.exp(scores - highest)
    totals = jnp.sum(expo, axis=-1, keepdims=True)
    log_total = highest + jnp.log(totals)
    probs_b = (expo / totals).astype(jnp.bfloat16)
    mixed = jnp.einsum("thqk,tkhd->tqhd", probs_b, values_all, preferred_element_type=jnp.float32)
    attended = mixed.reshape(tokens, D).astype(jnp.bfloat16)
    first_res = source + jnp.dot(attended, merge_w, preferred_element_type=jnp.float32)
    normed_two, inverse_two = normalize(first_res)
    h_second = (normed_two * gain_two).astype(jnp.bfloat16)
    expanded = jnp.dot(h_second, expand_w, preferred_element_type=jnp.float32)
    gate_val = expanded[:, :FF]
    up_val = expanded[:, FF:]

    def geglu(gate_in, up_in):
        return jax.nn.gelu(gate_in, approximate=False) * up_in

    activated, geglu_pull = jax.vjp(geglu, gate_val, up_val)
    hidden_b = activated.astype(jnp.bfloat16)
    result = (first_res + jnp.dot(hidden_b, shrink_w, preferred_element_type=jnp.float32)).astype(
        jnp.bfloat16
    )
    again = (
        lax.all_gather(first_gain, "fsdp", axis=0, tiled=True),
        lax.all_gather(joint_weight, "fsdp", axis=0, tiled=True),
        lax.all_gather(merge_weight, "fsdp", axis=0, tiled=True),
        lax.all_gather(second_gain, "fsdp", axis=0, tiled=True),
        lax.all_gather(expand_weight, "fsdp", axis=0, tiled=True),
        lax.all_gather(shrink_weight, "fsdp", axis=0, tiled=True),
    )
    gain_one = again[0].astype(jnp.float32)
    joint_w = again[1]
    merge_w = again[2]
    gain_two = again[3].astype(jnp.float32)
    expand_w = again[4]
    shrink_w = again[5]
    upstream = cotangent[0].astype(jnp.float32)
    upstream_b = cotangent[0]
    shrink_part = outer_sum(hidden_b, upstream_b)
    hidden_grad = back_product(upstream_b, shrink_w)
    gate_grad, up_grad = geglu_pull(hidden_grad)
    expand_in = jnp.concatenate([gate_grad, up_grad], axis=1).astype(jnp.bfloat16)
    expand_part = outer_sum(h_second, expand_in)
    second_up = back_product(expand_in, expand_w)
    res_back, second_part = norm_back(second_up, normed_two, inverse_two, gain_two)
    first_res_grad = upstream + res_back
    res_grad_b = first_res_grad.astype(jnp.bfloat16)
    merge_part = outer_sum(attended, res_grad_b)
    att_grad = (
        back_product(res_grad_b, merge_w)
        .astype(jnp.bfloat16)
        .reshape(tiles, tile_rows, HEADS, HEAD_DIM)
    )
    probs = jnp.exp(band_scores(queries_t, keys_all, offset, seq_length, rim_width) - log_total)
    prob_grad = jnp.einsum(
        "tqhd,tkhd->thqk", att_grad, values_all, preferred_element_type=jnp.float32
    )
    row_delta = jnp.sum(probs * prob_grad, axis=-1, keepdims=True)
    score_grad = (probs * (prob_grad - row_delta)).astype(jnp.bfloat16)
    query_grad = jnp.einsum(
        "thqk,tkhd->tqhd", score_grad, keys_all, preferred_element_type=jnp.float32
    ) * (1.0 / math.sqrt(HEAD_DIM))
    key_grad = jnp.einsum(
        "thqk,tqhd->tkhd", score_grad, queries_t, preferred_element_type=jnp.float32
    ) * (1.0 / math.sqrt(HEAD_DIM))
    value_grad = jnp.einsum(
        "thqk,tqhd->tkhd", probs_b, att_grad, preferred_element_type=jnp.float32
    )
    window_grad = jnp.concatenate(
        [key_grad.reshape(tiles, col_count, D), value_grad.reshape(tiles, col_count, D)], axis=2
    )
    lower_grad = window_grad[:, :tile_rows].reshape(tokens, 2 * D)
    upper_grad = window_grad[:, tile_rows:].reshape(tokens, 2 * D)
    pair_grad = jnp.pad(lower_grad, ((0, tile_rows), (0, 0))) + jnp.pad(
        upper_grad, ((tile_rows, 0), (0, 0))
    )
    from_before = passed_along(
        pair_grad[rim_width + tokens :].astype(jnp.bfloat16), "seq", 1
    ).astype(jnp.float32)
    from_after = passed_along(pair_grad[:rim_width].astype(jnp.bfloat16), "seq", -1).astype(
        jnp.float32
    )
    own_grad = pair_grad[rim_width : rim_width + tokens]
    own_grad = own_grad + jnp.pad(from_before, ((0, tokens - rim_width), (0, 0)))
    own_grad = own_grad + jnp.pad(from_after, ((tokens - rim_width, 0), (0, 0)))
    query_back = unrotate(query_grad.reshape(tokens, HEADS, HEAD_DIM), cosine, sine).reshape(
        tokens, D
    )
    key_back = unrotate(own_grad[:, :D].reshape(tokens, HEADS, HEAD_DIM), cosine, sine).reshape(
        tokens, D
    )
    joint_in = jnp.concatenate([query_back, key_back, own_grad[:, D:]], axis=1).astype(jnp.bfloat16)
    joint_part = outer_sum(h_first, joint_in)
    first_up = back_product(joint_in, joint_w)
    input_back, first_part = norm_back(first_up, normed_one, inverse_one, gain_one)
    input_grad = (first_res_grad + input_back).astype(jnp.bfloat16)
    parts = (first_part, joint_part, merge_part, second_part, expand_part, shrink_part)
    shares = (
        lax.psum_scatter(
            parts[0].astype(jnp.bfloat16), "fsdp", scatter_dimension=0, tiled=True
        ).astype(jnp.float32),
        lax.psum_scatter(
            parts[1].astype(jnp.bfloat16), "fsdp", scatter_dimension=0, tiled=True
        ).astype(jnp.float32),
        lax.psum_scatter(
            parts[2].astype(jnp.bfloat16), "fsdp", scatter_dimension=0, tiled=True
        ).astype(jnp.float32),
        lax.psum_scatter(
            parts[3].astype(jnp.bfloat16), "fsdp", scatter_dimension=0, tiled=True
        ).astype(jnp.float32),
        lax.psum_scatter(
            parts[4].astype(jnp.bfloat16), "fsdp", scatter_dimension=0, tiled=True
        ).astype(jnp.float32),
        lax.psum_scatter(
            parts[5].astype(jnp.bfloat16), "fsdp", scatter_dimension=0, tiled=True
        ).astype(jnp.float32),
    )
    totals_out = (
        lax.psum(shares[0].astype(jnp.bfloat16), "seq").astype(jnp.float32),
        lax.psum(shares[1].astype(jnp.bfloat16), "seq").astype(jnp.float32),
        lax.psum(shares[2].astype(jnp.bfloat16), "seq").astype(jnp.float32),
        lax.psum(shares[3].astype(jnp.bfloat16), "seq").astype(jnp.float32),
        lax.psum(shares[4].astype(jnp.bfloat16), "seq").astype(jnp.float32),
        lax.psum(shares[5].astype(jnp.bfloat16), "seq").astype(jnp.float32),
    )
    return (
        result[None],
        input_grad[None],
        totals_out[0],
        totals_out[1],
        totals_out[2],
        totals_out[3],
        totals_out[4],
        totals_out[5],
    )


def solution(mesh):
    placed = (
        P("fsdp", "seq", None),
        P("fsdp"),
        P("fsdp", None),
        P("fsdp", None),
        P("fsdp"),
        P("fsdp", None),
        P("fsdp", None),
        P("fsdp", "seq", None),
    )
    return jax.shard_map(
        shards,
        mesh=mesh,
        in_specs=placed,
        out_specs=(
            P("fsdp", "seq", None),
            P("fsdp", "seq", None),
            P("fsdp"),
            P("fsdp", None),
            P("fsdp", None),
            P("fsdp"),
            P("fsdp", None),
            P("fsdp", None),
        ),
        check_vma=False,
    )
```

profile of v0, /device:TPU:7, one launch (start us, length us, event | category | flops | bytes accessed | tf_op | source)
XLA Modules:
  0.0 721.5 jit_solution(8760715531091360105)
XLA Ops:
  13.4 18.1 %all-reduce.11 = (bf16[768]{0:T(1024)(128)(2,1)S(1)}, bf16[768]{0:T(1024)(128)(2,1)S(1)}) all-reduce(bf16[768]{0:T(1024)(128)(2,1)S(1)} %dynamic-update-slice, bf16[768]{0:T(1024)(128)(2,1)S(1)} %dynamic-update-slice.1), channel_id=1, replica_groups=mesh['fsdp'=8,'seq'=16] {'fsdp'}, use_global_device_ids=true, to_apply=%add.4 | all-reduce | flops 1536 | bytes 6144
  32.0 44.7 %all-gather.5.cloned.1.call-done = bf16[768,2304]{1,0:T(8,128)(2,1)} async-done(((bf16[96,2304]{1,0:T(8,128)(2,1)}), bf16[768,2304]{1,0:T(8,128)(2,1)}) %all-gather.5.cloned.1.call-update) | async-done | bytes 3538960 | tf_op jit(solution)/shard_map/all_gather | solution.py:127
  76.7 3.6 fusion.56
  82.0 1.6 copy.36
  84.5 3.7 collective-permute-start.1
  88.2 3.0 collective-permute-start
  96.9 3.3 fusion.2
  100.9 3.9 fusion
  105.0 2.7 divide_convert_fusion
  110.1 16.7 %all-gather.7.cloned.1.call-done = bf16[768,768]{1,0:T(8,128)(2,1)} async-done(((bf16[96,768]{1,0:T(8,128)(2,1)}), bf16[768,768]{1,0:T(8,128)(2,1)}) %all-gather.7.cloned.1.call-update) | async-done | bytes 1179664 | tf_op jit(solution)/shard_map/all_gather | solution.py:128
  126.9 2.4 fusion.63
  130.2 63.8 %all-gather.9.cloned.1.call-done = bf16[768,2304]{1,0:T(8,128)(2,1)} async-done(((bf16[96,2304]{1,0:T(8,128)(2,1)}), bf16[768,2304]{1,0:T(8,128)(2,1)}) %all-gather.9.cloned.1.call-update) | async-done | bytes 3538960 | tf_op jit(solution)/shard_map/all_gather | solution.py:130
  194.0 5.4 fusion.58
  199.4 47.3 %all-gather.11.cloned.1.call-done = bf16[1152,768]{1,0:T(8,128)(2,1)} async-done(((bf16[144,768]{1,0:T(8,128)(2,1)}), bf16[1152,768]{1,0:T(8,128)(2,1)}) %all-gather.11.cloned.1.call-update) | async-done | bytes 1769488 | tf_op jit(solution)/shard_map/all_gather | solution.py:131
  246.7 7.3 %add_convert_fusion = (bf16[384,1152]{1,0:T(8,128)(2,1)S(1)}, f32[384,1152]{1,0:T(8,128)S(1)}, f32[384,1152]{1,0:T(8,128)S(1)}) fusion(f32[384,2304]{1,0:T(8,128)} %fusion.58, bf16[1152,768]{1,0:T(8,128)(2,1)} %all-gather.11.cloned.1.call-done, bf16[1,384,768]{2,1,0:T(8,128)(2,1)} %param.15), kind=kOutput, calls=%fused_computation.29 | convolution fusion | flops 711770112 | bytes 10321920 | tf_op jit(solution)/shard_map/dot_general | solution.py:44
  255.4 1.6 copy-done.38
  257.1 2.3 multiply_reduce_fusion.1
  259.4 1.8 multiply_add_fusion
  261.2 1.8 convolution_convert_fusion.3
  263.3 3.7 convolution_convert_fusion.2
  267.0 5.7 convolution_convert_fusion
  272.8 2.8 convolution_convert_fusion.4
  275.7 2.8 reshape.222
  278.5 2.6 copy.45
  281.1 2.9 fusion.64
  284.0 3.2 copy.49
  287.3 3.9 multiply_reduce_fusion
  291.3 1.7 multiply_convert_fusion
  293.0 1.9 convolution_multiply_fusion
  294.9 3.1 copy.48
  297.9 5.1 pad_maximum_fusion
  303.1 3.1 copy.51
  306.1 3.1 copy.50
  309.2 2.7 fusion.1
  312.2 5.6 collective-permute-start.2
  317.8 2.2 collective-permute-start.3
  322.5 4.8 collective-permute-done.3
  331.1 4.0 convolution_convert_fusion.1
  336.3 3.5 fusion.25
  339.8 75.3 %reduce-scatter.11.cloned.1.call-done = bf16[144,768]{1,0:T(8,128)(2,1)} async-done(((bf16[1152,768]{1,0:T(8,128)(2,1)}), bf16[144,768]{1,0:T(8,128)(2,1)}) %reduce-scatter.11.cloned.1.call-update) | async-done | bytes 221200 | tf_op jit(solution)/shard_map/reduce_scatter | solution.py:278
  415.2 85.3 %reduce-scatter.9.cloned.1.call-done = bf16[96,2304]{1,0:T(8,128)(2,1)} async-done(((bf16[768,2304]{1,0:T(8,128)(2,1)}), bf16[96,2304]{1,0:T(8,128)(2,1)}) %reduce-scatter.9.cloned.1.call-update) | async-done | bytes 442384 | tf_op jit(solution)/shard_map/reduce_scatter | solution.py:275
  500.5 84.8 %reduce-scatter.5.cloned.1.call-done = bf16[96,2304]{1,0:T(8,128)(2,1)} async-done(((bf16[768,2304]{1,0:T(8,128)(2,1)}), bf16[96,2304]{1,0:T(8,128)(2,1)}) %reduce-scatter.5.cloned.1.call-update) | async-done | bytes 442384 | tf_op jit(solution)/shard_map/reduce_scatter | solution.py:266
  585.3 4.9 fusion.32
  590.2 14.8 %all-reduce.10 = (bf16[768]{0:T(1024)(128)(2,1)S(1)}, bf16[768]{0:T(1024)(128)(2,1)S(1)}) all-reduce(bf16[768]{0:T(1024)(128)(2,1)} %get-tuple-element.10, bf16[768]{0:T(1024)(128)(2,1)S(1)} %copy-done.37), channel_id=2, replica_groups=mesh['fsdp'=8,'seq'=16] {'fsdp'}, use_global_device_ids=true, to_apply=%region_12.13.clone | all-reduce | flops 1536 | bytes 6144
  605.2 32.2 %all-reduce.8 = (bf16[96]{0:T(256)(128)(2,1)S(1)}, bf16[96]{0:T(256)(128)(2,1)S(1)}) all-reduce(bf16[96]{0:T(256)(128)(2,1)S(1)} %dynamic-slice.3, bf16[96]{0:T(256)(128)(2,1)S(1)} %dynamic-slice.5), channel_id=1, replica_groups=mesh['fsdp'=8,'seq'=16] {'seq'}, use_global_device_ids=true, to_apply=%region_13.14 | all-reduce | flops 192 | bytes 768 | tf_op jit(solution)/shard_map/psum | solution.py:283
  641.0 68.5 %all-reduce.14.cloned.1.call-done = (bf16[96,2304]{1,0:T(8,128)(2,1)}, bf16[96,768]{1,0:T(8,128)(2,1)}, bf16[96,2304]{1,0:T(8,128)(2,1)}, bf16[144,768]{1,0:T(8,128)(2,1)}) async-done(((bf16[96,2304]{1,0:T(8,128)(2,1)}, bf16[96,768]{1,0:T(8,128)(2,1)}, bf16[96,2304]{1,0:T(8,128)(2,1)}, bf16[144,768]{1,0:T(8,128)(2,1)}), (bf16[96,2304]{1,0:T(8,128)(2,1)}, bf16[96,768]{1,0:T(8,128)(2,1)}, ...) | async-done | bytes 1253392 | tf_op jit(solution)/shard_map/psum | solution.py:284
  709.5 1.7 convert_element_type.154
  711.2 2.0 convert_element_type.152
  (166 shorter events, 32.3 us)
Async XLA Ops:
  7.2 4.5 copy-start.36
  7.2 4.2 copy-start.8
  7.2 5.8 copy-start.39
  7.2 6.0 copy-start.40
  7.2 69.5 %all-gather.5.cloned.1.call-start = ((), (), s32[]{:S(2)}) async-start(), calls=%async_computation.4 | async-start | bytes 3981312 | tf_op jit(solution)/shard_map/all_gather | solution.py:127
  7.9 118.9 %all-gather.7.cloned.1.call-start = ((), (), s32[]{:S(2)}) async-start(), calls=%async_computation.5 | async-start | bytes 1327104 | tf_op jit(solution)/shard_map/all_gather | solution.py:128
  8.7 185.3 %all-gather.9.cloned.1.call-start = ((), (), s32[]{:S(2)}) async-start(), calls=%async_computation.6 | async-start | bytes 3981312 | tf_op jit(solution)/shard_map/all_gather | solution.py:130
  9.4 237.3 %all-gather.11.cloned.1.call-start = ((), (), s32[]{:S(2)}) async-start(), calls=%async_computation.7 | async-start | bytes 1990656 | tf_op jit(solution)/shard_map/all_gather | solution.py:131
  10.0 329.8 %reduce-scatter.7.cloned.1.call-start = ((), (), s32[]{:S(2)}) async-start(), calls=%async_computation.9 | async-start | bytes 1327104 | tf_op jit(solution)/shard_map/reduce_scatter | solution.py:269
  11.7 68.7 %copy-start.33 = (f32[384]{0:T(512)}, f32[384]{0:T(512)S(1)}, u32[]{:S(2)}) copy-start(f32[384]{0:T(512)S(1)} %add_rsqrt_fusion.1) | copy-start | bytes 4612
  31.8 51.9 %copy-start.23 = (f32[384,32]{0,1:T(8,128)}, f32[384,32]{0,1:T(8,128)S(1)}, u32[]{:S(2)}) copy-start(f32[384,32]{0,1:T(8,128)S(1)} %get-tuple-element.52) | copy-start | bytes 147460
  31.8 51.9 %copy-start.25 = (f32[384,32]{0,1:T(8,128)}, f32[384,32]{0,1:T(8,128)S(1)}, u32[]{:S(2)}) copy-start(f32[384,32]{0,1:T(8,128)S(1)} %get-tuple-element.53) | copy-start | bytes 147460
  32.0 68.9 %copy-start.14 = (pred[3,128,256]{2,1,0:T(8,128)(4,1)}, pred[3,128,256]{2,1,0:T(8,128)(4,1)S(1)}, u32[]{:S(2)}) copy-start(pred[3,128,256]{2,1,0:T(8,128)(4,1)S(1)} %fusion.46) | copy-start | bytes 294916
  84.5 8.1 %collective-permute-start.1 = (bf16[64,1536]{1,0:T(8,128)(2,1)S(1)}, bf16[64,1536]{1,0:T(8,128)(2,1)S(1)}, u32[]{:S(2)}, u32[]{:S(2)}) collective-permute-start(bf16[64,1536]{1,0:T(8,128)(2,1)S(1)} %get-tuple-element.46), channel_id=1, source_target_pairs={{1,0},{2,1},{3,2},{4,3},{5,4},{6,5},{7,6},{8,7},{9,8},{10,9},{11,1... | collective-permute-start | bytes 589832 | tf_op jit(solution)/shard_map/ppermute | solution.py:26
  88.2 5.6 collective-permute-start
  91.3 5.5 copy-start.10
  96.8 3.3 copy-start.3
  100.8 7.0 copy-start.5
  100.8 4.2 copy-start
  105.0 2.8 copy-start.30
  129.3 126.2 %copy-start.12 = (f32[384,768]{1,0:T(8,128)}, f32[384,768]{1,0:T(8,128)S(1)}, u32[]{:S(2)}) copy-start(f32[384,768]{1,0:T(8,128)S(1)} %get-tuple-element.59) | copy-start | bytes 3538948
  246.7 7.3 %copy-start.17 = (f32[384,2304]{1,0:T(8,128)S(1)}, f32[384,2304]{1,0:T(8,128)}, u32[]{:S(2)}) copy-start(f32[384,2304]{1,0:T(8,128)} %fusion.58) | copy-start | bytes 10616836
  254.1 3.0 copy-start.38
  255.4 3.9 copy-start.19
  257.1 2.3 copy-start.20
  259.4 1.8 copy-start.18
  263.0 152.2 %reduce-scatter.11.cloned.1.call-start = ((), (), s32[]{:S(2)}) async-start(), calls=%async_computation.11 | async-start | bytes 1990656 | tf_op jit(solution)/shard_map/reduce_scatter | solution.py:278
  267.0 233.5 %reduce-scatter.9.cloned.1.call-start = ((), (), s32[]{:S(2)}) async-start(), calls=%async_computation.10 | async-start | bytes 3981312 | tf_op jit(solution)/shard_map/reduce_scatter | solution.py:275
  272.8 312.4 %reduce-scatter.5.cloned.1.call-start = ((), (), s32[]{:S(2)}) async-start(), calls=%async_computation.8 | async-start | bytes 3981312 | tf_op jit(solution)/shard_map/reduce_scatter | solution.py:266
  284.0 3.3 copy-start.29
  284.0 3.3 copy-start.31
  284.0 3.3 copy-start.6
  284.0 3.3 copy-start.7
  284.0 3.3 copy-start.15
  287.3 4.0 slice-start
  287.3 3.9 slice-start.1
  287.3 3.9 copy-start.16
  312.0 8.0 %copy-start.4 = (bf16[3,256,768]{1,2,0:T(8,128)(2,1)S(1)}, bf16[3,256,768]{1,2,0:T(8,128)(2,1)}, u32[]{:S(2)}) copy-start(bf16[3,256,768]{1,2,0:T(8,128)(2,1)} %copy-done.3) | copy-start | bytes 3538948
  312.2 10.3 %collective-permute-start.2 = (bf16[64,1536]{0,1:T(8,128)(2,1)S(1)}, bf16[64,1536]{0,1:T(8,128)(2,1)S(1)}, u32[]{:S(2)}, u32[]{:S(2)}) collective-permute-start(bf16[64,1536]{0,1:T(8,128)(2,1)S(1)} %get-tuple-element.34), channel_id=1, source_target_pairs={{0,1},{1,2},{2,3},{3,4},{4,5},{5,6},{6,7},{7,8},{8,9},{9,10},{10,1... | collective-permute-start | bytes 589832 | tf_op jit(solution)/shard_map/ppermute | solution.py:34
  317.8 9.5 %collective-permute-start.3 = (bf16[64,1536]{0,1:T(8,128)(2,1)S(1)}, bf16[64,1536]{0,1:T(8,128)(2,1)S(1)}, u32[]{:S(2)}, u32[]{:S(2)}) collective-permute-start(bf16[64,1536]{0,1:T(8,128)(2,1)S(1)} %get-tuple-element.35), channel_id=1, source_target_pairs={{1,0},{2,1},{3,2},{4,3},{5,4},{6,5},{7,6},{8,7},{9,8},{10,9},{11,1... | collective-permute-start | bytes 589832 | tf_op jit(solution)/shard_map/ppermute | solution.py:34
  320.0 7.3 %copy-start.2 = (f32[384,1536]{0,1:T(8,128)S(1)}, f32[384,1536]{0,1:T(8,128)}, u32[]{:S(2)}) copy-start(f32[384,1536]{0,1:T(8,128)} %copy.50) | copy-start | bytes 7077892
  320.9 6.3 copy-start.1
  329.9 5.1 copy-start.21
  330.0 5.0 copy-start.22
  335.1 374.4 %all-reduce.14.cloned.1.call-start = ((), (), s32[]{:S(2)}) async-start(), calls=%async_computation.12 | async-start | bytes 2506752 | tf_op jit(solution)/shard_map/psum | solution.py:284
  585.2 4.9 copy-start.37
  709.5 3.7 copy-start.32
  709.5 4.5 copy-start.27
  (9 other events, 10.4 us)
Sparse Core Ops, SparseCore 0:
  10.4 66.3 all-gather.4
  79.0 47.7 all-gather.6
  129.2 64.7 all-gather.8
  196.2 50.5 all-gather.10
  263.1 71.7 reduce-scatter.6
  339.0 76.1 reduce-scatter.10
  419.7 80.7 reduce-scatter.8
  504.4 80.7 reduce-scatter.4
  588.2 121.2 all-reduce.13
where the time goes:
time: 724 us; the launch traced here: 722 us
  waiting for transfers between devices  498 us (69%)
  blocking collectives  65.2 us (9%)
  matrix products  61.4 us (8%)
  other arithmetic  35 us (5%)
  local copies, waits for them, and re-layouts  31 us (4%)
  between operations  16 us (2%)
  starting transfers between devices  15.1 us (2%)
    reduce_scatter x1, waiting for transfers between devices, shards(): lax.psum_scatter(parts[4].astype(jnp.bfloat16), 'fsdp', scatter_dimension...  85.3 us
    reduce_scatter x1, waiting for transfers between devices, shards(): lax.psum_scatter(parts[1].astype(jnp.bfloat16), 'fsdp', scatter_dimension...  84.8 us
    reduce_scatter x1, waiting for transfers between devices, shards(): lax.psum_scatter(parts[5].astype(jnp.bfloat16), 'fsdp', scatter_dimension...  75.3 us
    psum x1, waiting for transfers between devices, shards(): lax.psum(shares[1].astype(jnp.bfloat16), 'seq').astype(jnp.float32)  68.5 us
    all_gather x1, waiting for transfers between devices, shards(): lax.all_gather(expand_weight, 'fsdp', axis=0, tiled=True)  63.8 us
    all_gather x1, waiting for transfers between devices, shards(): lax.all_gather(shrink_weight, 'fsdp', axis=0, tiled=True)  47.3 us
    all_gather x1, waiting for transfers between devices, shards(): lax.all_gather(joint_weight, 'fsdp', axis=0, tiled=True)  44.7 us
    unnamed x2, blocking collectives  32.9 us
  transfers between devices with their start and end apart: 13, of which 12 were waited for; matrix products, arithmetic and copies ran while one was open for 14% of the time, Pallas kernels for 0%

commit v1 on v0

v1 whole, which is shorter than its diff:
```python
import math

import jax
import jax.numpy as jnp
from jax import lax
from jax.sharding import PartitionSpec as P

D = 768
HEADS = 12
HEAD_DIM = 64
FF = 1152
WINDOW = 128
RIM = WINDOW // 2
EPSILON = 1e-05
F32 = jnp.float32
BF16 = jnp.bfloat16


def over_fsdp(value, dx, dz):
    pairs = [
        (x * 2 + z, ((x + dx) % 4) * 2 + (z + dz) % 2) for x in range(4) for z in range(2)
    ]
    return lax.ppermute(value, "fsdp", pairs)


def over_seq(value, dz, dy, dc):
    pairs = [
        (z * 8 + y * 2 + c, ((z + dz) % 2) * 8 + ((y + dy) % 4) * 2 + (c + dc) % 2)
        for z in range(2)
        for y in range(4)
        for c in range(2)
    ]
    return lax.ppermute(value, "seq", pairs)


def core_swap(value):
    return over_seq(value, 0, 0, 1)


def passed_along(value, steps):
    first, last = (max(0, -steps), min(16, 16 - steps))
    return lax.ppermute(value, "seq", [(i, i + steps) for i in range(first, last)])


def gather_pieces(own):
    from_low = over_fsdp(own, 1, 0)
    from_high = over_fsdp(own, -1, 0)
    across = over_fsdp(own, 0, 1)
    from_far = over_fsdp(own, 2, 0)
    across_low = over_fsdp(across, 1, 0)
    across_high = over_fsdp(across, -1, 0)
    across_far = over_fsdp(from_far, 0, 1)
    return [own, across, from_high, across_high, from_far, across_far, from_low, across_low]


def assembled(pieces, core, x, zh):
    mine = jnp.stack(pieces)
    other = core_swap(mine)
    halves = jnp.where(core == 0, jnp.stack([mine, other], 1), jnp.stack([other, mine], 1))
    rel = halves.reshape((4, 2) + halves.shape[1:])
    rel = jnp.where(zh == 0, rel, rel[:, ::-1])
    twice = jnp.concatenate([rel, rel], 0)
    out = lax.dynamic_slice_in_dim(twice, (4 - x) % 4, 4, 0)
    return out.reshape((8,) + halves.shape[1:])


def spread_sum(parts, x, zh):
    by_x = parts.reshape((4, 2) + parts.shape[1:])

    def block(dx):
        return lax.dynamic_index_in_dim(by_x, (x + dx) % 4, 0, keepdims=False)

    got = [over_fsdp(block(d), d, 0) for d in (1, -1, 2)]
    total = block(0).astype(F32) + sum(g.astype(F32) for g in got)
    total = total.astype(BF16)
    keep = jnp.where(zh == 0, total[0], total[1])
    give = jnp.where(zh == 0, total[1], total[0])
    total = (keep.astype(F32) + over_fsdp(give, 0, 1).astype(F32)).astype(BF16)
    low, high, far = (over_seq(total, 0, d, 0) for d in (1, -1, 2))
    total = (
        (total.astype(F32) + far.astype(F32)) + (low.astype(F32) + high.astype(F32))
    ).astype(BF16)
    return (total.astype(F32) + over_seq(total, 1, 0, 0).astype(F32)).astype(BF16)


def outer_sum(left, right):
    return lax.dot_general(
        left, right, (((0,), (0,)), ((), ())), preferred_element_type=jnp.float32
    )


def back_product(left, weight):
    return lax.dot_general(
        left, weight, (((1,), (1,)), ((), ())), preferred_element_type=jnp.float32
    )


def normalize(values):
    centred = values - jnp.mean(values, axis=-1, keepdims=True)
    spread = jnp.mean(centred * centred, axis=-1, keepdims=True)
    inverse = lax.rsqrt(spread + EPSILON)
    return (centred * inverse, inverse)


def norm_back(upstream, normed, inverse, gain):
    gain_part = jnp.sum(upstream * normed, axis=0)
    scaled = upstream * gain
    centred = scaled - jnp.mean(scaled, axis=-1, keepdims=True)
    return (
        inverse * (centred - normed * jnp.mean(scaled * normed, axis=-1, keepdims=True)),
        gain_part,
    )


def rotate(values, cosine, sine):
    middle = values.shape[-1] // 2
    former = values[..., :middle]
    latter = values[..., middle:]
    return jnp.concatenate(
        [former * cosine - latter * sine, latter * cosine + former * sine], axis=-1
    )


def unrotate(upstream, cosine, sine):
    return rotate(upstream, cosine, -sine)


def band_windows(extended, tokens, tile_rows):
    tiles = tokens // tile_rows
    lower = extended[:tokens].reshape(tiles, tile_rows, extended.shape[1])
    upper = extended[tile_rows : tokens + tile_rows].reshape(tiles, tile_rows, extended.shape[1])
    return jnp.concatenate([lower, upper], axis=1)


def band_scores(queries, keys_all, offset, seq_length):
    scores = jnp.einsum(
        "tqhd,tkhd->thqk", queries, keys_all, preferred_element_type=jnp.float32
    ) * (1.0 / math.sqrt(HEAD_DIM))
    shape = (queries.shape[0], queries.shape[1], keys_all.shape[1])
    query_pos = lax.broadcasted_iota(jnp.int32, shape, 1)
    key_pos = lax.broadcasted_iota(jnp.int32, shape, 2) - RIM
    tile_base = lax.broadcasted_iota(jnp.int32, shape, 0) * queries.shape[1]
    global_key = offset + tile_base + key_pos
    allowed = (
        (jnp.abs(query_pos - key_pos) <= RIM) & (global_key >= 0) & (global_key < seq_length)
    )
    return jnp.where(allowed[:, None], scores, -1e30)


def column_half(value, core):
    width = value.shape[1] // 2
    mine = lax.dynamic_slice_in_dim(value, core * width, width, 1)
    other = lax.dynamic_slice_in_dim(value, (1 - core) * width, width, 1)
    return mine, other


def pair_outer(left, right, core):
    mine, give = column_half(right, core)
    got = core_swap(give)
    left_other = core_swap(left)
    return outer_sum(left, mine) + outer_sum(left_other, got)


def joined(total, core):
    other = core_swap(total)
    return jnp.where(
        core == 0,
        jnp.concatenate([total, other], 1),
        jnp.concatenate([other, total], 1),
    ).astype(F32)


def shards(
    inputs,
    first_gain,
    joint_weight,
    merge_weight,
    second_gain,
    expand_weight,
    shrink_weight,
    cotangent,
):
    tokens = inputs.shape[1]
    tile_rows = 2 * RIM
    tiles = tokens // tile_rows
    fsdp, seq = lax.axis_index("fsdp"), lax.axis_index("seq")
    x, zh, core = fsdp // 2, fsdp % 2, seq % 2
    offset = seq * tokens
    seq_length = tokens * 16
    rows = joint_weight.shape[0]

    def half(w):
        n = w.shape[0] // 2
        return lax.dynamic_slice_in_dim(w, core * n, n, 0)

    gains = jnp.zeros((rows // 2, 128), BF16)
    gains = gains.at[0, :rows].set(first_gain).at[1, :rows].set(second_gain)
    first_group = gather_pieces(jnp.concatenate([half(joint_weight), gains], 1))
    low_halo = passed_along(inputs[0, tokens - RIM :], 1)
    high_halo = passed_along(inputs[0, :RIM], -1)
    first_all = assembled(first_group, core, x, zh)
    joint_w = first_all[:, :, :, : 3 * D].reshape(D, 3 * D)
    gain_one = first_all[:, 0, 0, 3 * D : 3 * D + rows].reshape(D).astype(F32)
    gain_two = first_all[:, 0, 1, 3 * D : 3 * D + rows].reshape(D).astype(F32)
    expand_h = half(expand_weight)
    second_own = jnp.concatenate(
        [half(merge_weight)]
        + [expand_h[:, i * D : (i + 1) * D] for i in range(3)]
        + [half(shrink_weight)],
        0,
    )
    second_all = assembled(gather_pieces(second_own), core, x, zh)
    hr = rows // 2
    merge_w = second_all[:, :, :hr].reshape(D, D)
    expand_w = jnp.concatenate(
        [second_all[:, :, hr * (i + 1) : hr * (i + 2)].reshape(D, D) for i in range(3)], 1
    )
    shrink_w = second_all[:, :, hr * 4 :].reshape(FF, D)

    frequencies = jnp.exp(
        jnp.arange(HEAD_DIM // 2, dtype=jnp.float32) * (-2.0 * math.log(10000.0) / HEAD_DIM)
    )
    wide = tokens + 2 * RIM
    positions = (offset - RIM + lax.iota(jnp.int32, wide)).astype(jnp.float32)
    angles = positions[:, None] * frequencies[None, :]
    cosine = jnp.cos(angles)[:, None, :]
    sine = jnp.sin(angles)[:, None, :]
    own = slice(RIM, RIM + tokens)
    extended = jnp.concatenate([low_halo, inputs[0], high_halo], 0).astype(F32)
    source = inputs[0].astype(jnp.float32)
    normed_one, inverse_one = normalize(extended)
    h_first = (normed_one * gain_one).astype(jnp.bfloat16)
    joint = jnp.dot(h_first, joint_w, preferred_element_type=jnp.float32)
    queries = rotate(
        joint[own, :D].reshape(tokens, HEADS, HEAD_DIM), cosine[own], sine[own]
    ).astype(jnp.bfloat16)
    keys_rot = rotate(joint[:, D : 2 * D].reshape(wide, HEADS, HEAD_DIM), cosine, sine).astype(
        jnp.bfloat16
    )
    values_b = joint[:, 2 * D :].astype(jnp.bfloat16)
    paired = jnp.concatenate([keys_rot.reshape(wide, D), values_b], axis=1)
    windows = band_windows(paired, tokens, tile_rows)
    col_count = windows.shape[1]
    keys_all = windows[:, :, :D].reshape(tiles, col_count, HEADS, HEAD_DIM)
    values_all = windows[:, :, D:].reshape(tiles, col_count, HEADS, HEAD_DIM)
    queries_t = queries.reshape(tiles, tile_rows, HEADS, HEAD_DIM)
    scores = band_scores(queries_t, keys_all, offset, seq_length)
    highest = jnp.max(scores, axis=-1, keepdims=True)
    expo = jnp.exp(scores - highest)
    totals = jnp.sum(expo, axis=-1, keepdims=True)
    log_total = highest + jnp.log(totals)
    probs_b = (expo / totals).astype(jnp.bfloat16)
    mixed = jnp.einsum("thqk,tkhd->tqhd", probs_b, values_all, preferred_element_type=jnp.float32)
    attended = mixed.reshape(tokens, D).astype(jnp.bfloat16)
    first_res = source + jnp.dot(attended, merge_w, preferred_element_type=jnp.float32)
    normed_two, inverse_two = normalize(first_res)
    h_second = (normed_two * gain_two).astype(jnp.bfloat16)
    expanded = jnp.dot(h_second, expand_w, preferred_element_type=jnp.float32)
    gate_val = expanded[:, :FF]
    up_val = expanded[:, FF:]

    def geglu(gate_in, up_in):
        return jax.nn.gelu(gate_in, approximate=False) * up_in

    activated, geglu_pull = jax.vjp(geglu, gate_val, up_val)
    hidden_b = activated.astype(jnp.bfloat16)
    result = (first_res + jnp.dot(hidden_b, shrink_w, preferred_element_type=jnp.float32)).astype(
        jnp.bfloat16
    )
    upstream = cotangent[0].astype(jnp.float32)
    upstream_b = cotangent[0]
    shrink_part = pair_outer(hidden_b, upstream_b, core)
    hidden_grad = back_product(upstream_b, shrink_w)
    gate_grad, up_grad = geglu_pull(hidden_grad)
    expand_in = jnp.concatenate([gate_grad, up_grad], axis=1).astype(jnp.bfloat16)
    expand_part = pair_outer(h_second, expand_in, core)
    second_up = back_product(expand_in, expand_w)
    res_back, second_part = norm_back(second_up, normed_two, inverse_two, gain_two)
    first_res_grad = upstream + res_back
    res_grad_b = first_res_grad.astype(jnp.bfloat16)
    merge_part = pair_outer(attended, res_grad_b, core)
    early = jnp.concatenate(
        [
            merge_part.reshape(8, rows, D // 2),
            expand_part[:, :384].reshape(8, rows, D // 2),
            expand_part[:, 384:768].reshape(8, rows, D // 2),
            expand_part[:, 768:].reshape(8, rows, D // 2),
            shrink_part.reshape(8, -1, D // 2),
        ],
        1,
    ).astype(BF16)
    early_sum = joined(spread_sum(early, x, zh), core)
    att_grad = (
        back_product(res_grad_b, merge_w)
        .astype(jnp.bfloat16)
        .reshape(tiles, tile_rows, HEADS, HEAD_DIM)
    )
    probs = jnp.exp(band_scores(queries_t, keys_all, offset, seq_length) - log_total)
    prob_grad = jnp.einsum(
        "tqhd,tkhd->thqk", att_grad, values_all, preferred_element_type=jnp.float32
    )
    row_delta = jnp.sum(probs * prob_grad, axis=-1, keepdims=True)
    score_grad = (probs * (prob_grad - row_delta)).astype(jnp.bfloat16)
    query_grad = jnp.einsum(
        "thqk,tkhd->tqhd", score_grad, keys_all, preferred_element_type=jnp.float32
    ) * (1.0 / math.sqrt(HEAD_DIM))
    key_grad = jnp.einsum(
        "thqk,tqhd->tkhd", score_grad, queries_t, preferred_element_type=jnp.float32
    ) * (1.0 / math.sqrt(HEAD_DIM))
    value_grad = jnp.einsum(
        "thqk,tqhd->tkhd", probs_b, att_grad, preferred_element_type=jnp.float32
    )
    window_grad = jnp.concatenate(
        [key_grad.reshape(tiles, col_count, D), value_grad.reshape(tiles, col_count, D)], axis=2
    )
    lower_grad = window_grad[:, :tile_rows].reshape(tokens, 2 * D)
    upper_grad = window_grad[:, tile_rows:].reshape(tokens, 2 * D)
    pair_grad = jnp.pad(lower_grad, ((0, tile_rows), (0, 0))) + jnp.pad(
        upper_grad, ((tile_rows, 0), (0, 0))
    )
    query_back = unrotate(
        query_grad.reshape(tokens, HEADS, HEAD_DIM), cosine[own], sine[own]
    ).reshape(tokens, D)
    query_back = jnp.pad(query_back, ((RIM, RIM), (0, 0)))
    key_back = unrotate(pair_grad[:, :D].reshape(wide, HEADS, HEAD_DIM), cosine, sine).reshape(
        wide, D
    )
    joint_in = jnp.concatenate([query_back, key_back, pair_grad[:, D:]], axis=1).astype(
        jnp.bfloat16
    )
    joint_part = pair_outer(h_first, joint_in, core)
    first_up = back_product(joint_in, joint_w)
    input_back, first_part = norm_back(first_up, normed_one, inverse_one, gain_one)
    gain_rows = jnp.zeros((8, rows, 128), F32)
    gain_rows = gain_rows.at[:, 0, :rows].set(first_part.reshape(8, rows))
    gain_rows = gain_rows.at[:, 1, :rows].set(second_part.reshape(8, rows))
    late = jnp.concatenate([joint_part.reshape(8, rows, -1), gain_rows], 2).astype(BF16)
    late_sum = spread_sum(late, x, zh)
    gain_mine = late_sum[:2, 3 * D // 2 :].astype(F32)
    late_other = core_swap(late_sum)
    gain_other = late_other[:2, 3 * D // 2 :].astype(F32)
    gain_sum = gain_mine + gain_other
    a, b = late_sum[:, : 3 * D // 2], late_other[:, : 3 * D // 2]
    joint_grad = jnp.where(
        core == 0, jnp.concatenate([a, b], 1), jnp.concatenate([b, a], 1)
    ).astype(F32)
    to_low = passed_along(input_back[:RIM].astype(BF16), -1).astype(F32)
    to_high = passed_along(input_back[RIM + tokens :].astype(BF16), 1).astype(F32)
    input_back = (
        input_back[own]
        + jnp.pad(to_low, ((tokens - RIM, 0), (0, 0)))
        + jnp.pad(to_high, ((0, tokens - RIM), (0, 0)))
    )
    input_grad = (first_res_grad + input_back).astype(jnp.bfloat16)
    merge_grad = early_sum[:rows]
    expand_grad = jnp.concatenate(
        [early_sum[rows * (i + 1) : rows * (i + 2), :384] for i in range(3)]
        + [early_sum[rows * (i + 1) : rows * (i + 2), 384:] for i in range(3)],
        1,
    )
    shrink_grad = early_sum[rows * 4 :]
    return (
        result[None],
        input_grad[None],
        gain_sum[0, :rows],
        joint_grad,
        merge_grad,
        gain_sum[1, :rows],
        expand_grad,
        shrink_grad,
    )


def solution(mesh):
    placed = (
        P("fsdp", "seq", None),
        P("fsdp"),
        P("fsdp", None),
        P("fsdp", None),
        P("fsdp"),
        P("fsdp", None),
        P("fsdp", None),
        P("fsdp", "seq", None),
    )
    return jax.shard_map(
        shards,
        mesh=mesh,
        in_specs=placed,
        out_specs=(
            P("fsdp", "seq", None),
            P("fsdp", "seq", None),
            P("fsdp"),
            P("fsdp", None),
            P("fsdp", None),
            P("fsdp"),
            P("fsdp", None),
            P("fsdp", None),
        ),
        check_vma=False,
    )
```

time: 724 us -> 367 us (0.51)
  waiting for transfers between devices: 498 us -> 128 us
  blocking collectives: 65.2 us -> 0 us
  starting transfers between devices: 15.1 us -> 54.6 us
  local copies, waits for them, and re-layouts: 31 us -> 68.2 us
  other arithmetic: 35 us -> 54.1 us
  between operations: 16 us -> 2.48 us
  matrix products: 61.4 us -> 52.5 us
    reduce_scatter x4 -> x0, waiting for transfers between devices: 245 us -> none  [the longest x1 85.3 us: shards(): lax.psum_scatter(parts[4].astype(jnp.bfloat16), 'fsdp', scatter_dimension...]
    all_gather x4 -> x0, waiting for transfers between devices: 173 us -> none  [the longest x1 63.8 us: shards(): lax.all_gather(expand_weight, 'fsdp', axis=0, tiled=True)]
    ppermute x4 -> x46, waiting for transfers between devices: 8.74 us -> 128 us  [the longest x22 98.8 us: over_fsdp(): return lax.ppermute(value, 'fsdp', pairs)]
    psum x1 -> x0, waiting for transfers between devices: 68.5 us -> none  [shards(): lax.psum(shares[1].astype(jnp.bfloat16), 'seq').astype(jnp.float32)]
    ppermute x4 -> x46, starting transfers between devices: 14.5 us -> 54.6 us  [the longest x22 23.5 us: over_fsdp(): return lax.ppermute(value, 'fsdp', pairs)]
    unnamed x2 -> x0, blocking collectives: 32.9 us -> none
    psum x1 -> x0, blocking collectives: 32.2 us -> none  [shards(): lax.psum(shares[0].astype(jnp.bfloat16), 'seq').astype(jnp.float32)]
    unnamed x96 -> x144, local copies, waits for them, and re-layouts: 5.49 us -> 23.3 us
  transfers between devices with their start and end apart: 13 -> 46, of which waited for: 12 -> 19; matrix products, arithmetic and copies ran while one was open for 14% -> 44% of each run, Pallas kernels for 0% -> 0%
where the time goes in v1:
time: 367 us; the launch traced here: 360 us
  waiting for transfers between devices  128 us (35%)
  local copies, waits for them, and re-layouts  68.2 us (19%)
  starting transfers between devices  54.6 us (15%)
  other arithmetic  54.1 us (15%)
  matrix products  52.5 us (14%)
    ppermute x22, waiting for transfers between devices, over_fsdp(): return lax.ppermute(value, 'fsdp', pairs)  98.8 us
    ppermute x20, waiting for transfers between devices, over_seq(): return lax.ppermute(value, 'seq', pairs)  29.6 us
    ppermute x22, starting transfers between devices, over_fsdp(): return lax.ppermute(value, 'fsdp', pairs)  23.5 us
    unnamed x144, local copies, waits for them, and re-layouts  23.3 us
    ppermute x20, starting transfers between devices, over_seq(): return lax.ppermute(value, 'seq', pairs)  18.6 us
    dot_general x8, matrix products, outer_sum(): lax.dot_general(left, right, (((0,), (0,)), ((), ())), preferred_element_...  17.5 us
    ppermute x4, starting transfers between devices, passed_along(): lax.ppermute(value, 'seq', [(i, i + steps) for i in range(first, last)])  12.5 us
    dot_general x4, matrix products, back_product(): lax.dot_general(left, weight, (((1,), (1,)), ((), ())), preferred_element...  12.2 us
  transfers between devices with their start and end apart: 46, of which 19 were waited for; matrix products, arithmetic and copies ran while one was open for 44% of the time, Pallas kernels for 0%

profile of v1, /device:TPU:7, one launch (start us, length us, event | category | flops | bytes accessed | tf_op | source)
XLA Modules:
  0.0 360.3 jit_solution(1293476869735987892)
XLA Ops:
  8.4 3.6 collective-permute-start.10
  15.0 4.6 %collective-permute-start = (bf16[64,768]{1,0:T(8,128)(2,1)}, bf16[64,768]{1,0:T(8,128)(2,1)}, u32[]{:S(2)}, u32[]{:S(2)}) collective-permute-start(bf16[64,768]{1,0:T(8,128)(2,1)} %get-tuple-element.103), channel_id=1, source_target_pairs={{0,1},{1,2},{2,3},{3,4},{4,5},{5,6},{6,7},{7,8},{8,9},{9,10},{10,1... | collective-permute-start | bytes 294920 | tf_op jit(solution)/shard_map/ppermute | solution.py:42
  33.1 3.4 collective-permute-done.2
  39.0 6.4 %collective-permute-done.5 = bf16[48,2432]{1,0:T(8,128)(2,1)S(1)} collective-permute-done((bf16[48,2432]{1,0:T(8,128)(2,1)S(1)}, bf16[48,2432]{1,0:T(8,128)(2,1)S(1)}, u32[]{:S(2)}, u32[]{:S(2)}) %collective-permute-start.5) | collective-permute-done | bytes 233504 | tf_op jit(solution)/shard_map/ppermute | solution.py:23
  47.0 3.4 collective-permute-done.4
  50.4 8.2 %collective-permute-done.6 = bf16[48,2432]{1,0:T(8,128)(2,1)S(1)} collective-permute-done((bf16[48,2432]{1,0:T(8,128)(2,1)S(1)}, bf16[48,2432]{1,0:T(8,128)(2,1)S(1)}, u32[]{:S(2)}, u32[]{:S(2)}) %collective-permute-start.6) | collective-permute-done | bytes 233504 | tf_op jit(solution)/shard_map/ppermute | solution.py:23
  58.9 5.6 %collective-permute-done.7 = bf16[48,2432]{1,0:T(8,128)(2,1)S(1)} collective-permute-done((bf16[48,2432]{1,0:T(8,128)(2,1)S(1)}, bf16[48,2432]{1,0:T(8,128)(2,1)S(1)}, u32[]{:S(2)}, u32[]{:S(2)}) %collective-permute-start.7) | collective-permute-done | bytes 233504 | tf_op jit(solution)/shard_map/ppermute | solution.py:23
  66.1 3.4 collective-permute-done.8
  69.5 3.4 collective-permute-start.9
  79.6 5.8 %collective-permute-done.12 = bf16[264,768]{1,0:T(8,128)(2,1)S(1)} collective-permute-done((bf16[264,768]{1,0:T(8,128)(2,1)}, bf16[264,768]{1,0:T(8,128)(2,1)S(1)}, u32[]{:S(2)}, u32[]{:S(2)}) %collective-permute-start.12) | collective-permute-done | bytes 405536 | tf_op jit(solution)/shard_map/ppermute | solution.py:23
  88.6 8.7 %collective-permute-done.14 = bf16[264,768]{1,0:T(8,128)(2,1)S(1)} collective-permute-done((bf16[264,768]{1,0:T(8,128)(2,1)}, bf16[264,768]{1,0:T(8,128)(2,1)S(1)}, u32[]{:S(2)}, u32[]{:S(2)}) %collective-permute-start.14) | collective-permute-done | bytes 405536 | tf_op jit(solution)/shard_map/ppermute | solution.py:23
  107.8 4.3 %fusion.95 = f32[512,2304]{1,0:T(8,128)S(1)} fusion(bf16[512,768]{1,0:T(8,128)(2,1)S(1)} %fusion.25, bf16[768,2304]{1,0:T(8,128)(2,1)} %bitcast.231), kind=kOutput, calls=%fused_computation.262 | convolution fusion | flops 1811939328 | bytes 9043968 | tf_op jit(solution)/shard_map/dot_general | solution.py:233
  114.7 2.8 copy.28
  123.2 2.8 copy.27
  134.5 5.6 %maximum_select_fusion = bf16[4,2,2,264,768]{4,3,2,1,0:T(8,128)(2,1)S(1)} fusion(bf16[4,2,1,264,768]{4,3,2,1,0:T(8,128)(2,1)} %bitcast.40, bf16[4,2,1,264,768]{4,3,2,1,0:T(8,128)(2,1)} %bitcast.38, pred[]{:T(512)S(6)} %eq.28), kind=kLoop, calls=%fused_computation.6 | loop fusion | flops 9732096 | bytes 12976129 | tf_op jit(solution)/shard_map/jit(_where)/select_n | solution.py:59
  140.2 4.1 %reverse_select_fusion = bf16[4,2,2,264,768]{4,3,2,1,0:T(8,128)(2,1)} fusion(bf16[4,2,2,264,768]{4,3,2,1,0:T(8,128)(2,1)S(1)} %maximum_select_fusion, pred[]{:T(512)S(6)} %eq.27), kind=kLoop, calls=%fused_computation.2 | loop fusion | flops 3244032 | bytes 12976129 | tf_op jit(solution)/shard_map/jit(_where)/select_n | solution.py:61
  144.2 8.0 %fusion = bf16[4,2,2,264,768]{4,3,2,1,0:T(8,128)(2,1)} fusion(s32[]{:T(128)S(6)} %select_n.187, bf16[4,2,2,264,768]{4,3,2,1,0:T(8,128)(2,1)} %reverse_select_fusion), kind=kLoop, calls=%fused_computation.5 | loop fusion | flops 3244032 | bytes 12976132 | tf_op jit(solution)/shard_map/concatenate | solution.py:62
  152.2 2.6 fusion.91
  159.1 2.7 fusion.34
  161.8 4.4 %add_convert_fusion = (bf16[384,1152]{1,0:T(8,128)(2,1)S(1)}, f32[384,1152]{1,0:T(8,128)S(1)}, f32[384,1152]{1,0:T(8,128)S(1)}) fusion(f32[384,2304]{1,0:T(8,128)S(1)} %fusion.34, bf16[1152,768]{1,0:T(8,128)(2,1)S(1)} %bitcast.248, bf16[1,384,768]{2,1,0:T(8,128)(2,1)S(1)} %copy-done.35), kind=kOutput, calls=%fused_computation.59 | convolution fusion | flops 711770112 | bytes 10321920 | tf_op jit(solution)/shard_map/dot_general | solution.py:93
  167.6 2.3 multiply_reduce_fusion.2
  173.8 3.0 reshape.490
  176.7 2.6 copy.39
  179.3 3.1 fusion.96
  182.4 3.8 %multiply_reduce_fusion = (f32[3,12,128]{2,1,0:T(8,128)S(1)}, f32[3,12,128,256]{3,2,1,0:T(8,128)S(1)}) fusion(f32[3,12,128,256]{3,2,1,0:T(8,128)} %copy-done.2, f32[3,12,128]{2,1,0:T(8,128)S(1)} %log_add_fusion, pred[3,128,256]{2,1,0:T(8,128)(4,1)S(1)} %fusion.67, bf16[3,128,12,64]{1,3,2,0:T(8,128)(2,1)S(1)} %copy-done.17, ...), kind=kOutput, calls=%fused_computation.12 | convolution fusion | flops 156888576 | bytes 11341824 | tf_op jit(solution)/shard_map/tqhd,tkhd->thqk/dot_general | solution.py:299
  193.2 4.2 %fusion.49 = f32[768,1152]{1,0:T(8,128)} fusion(bf16[384,768]{1,0:T(8,128)(2,1)} %multiply_convert_fusion.3, s32[]{:T(128)S(6)} %select_n.195, bf16[384,1152]{1,0:T(8,128)(2,1)S(1)} %copy-done.33, bf16[384,1152]{1,0:T(8,128)(2,1)S(1)} %copy-done.16), kind=kOutput, calls=%fused_computation.129 | convolution fusion | flops 681246720 | bytes 5898244 | tf_op jit(solution)/shard_map/dot_general | solution.py:87
  199.3 3.2 copy.42
  202.5 4.5 %fusion.10 = (f32[3,128,1536]{2,1,0:T(8,128)}, f32[3,128,1536]{2,1,0:T(8,128)}) fusion(f32[3,256,768]{2,1,0:T(8,128)} %copy.42, f32[3,256,768]{2,1,0:T(8,128)S(1)} %copy-done.14), kind=kLoop, calls=%fused_computation.39 | loop fusion | flops 1179648 | bytes 9437184 | tf_op jit(solution)/shard_map/concatenate | solution.py:313
  209.0 3.1 copy.45
  217.2 3.0 fusion.45
  221.5 3.9 %fusion.29 = (bf16[768]{0:T(1024)(128)(2,1)S(1)}, f32[512]{0:T(512)S(1)}, f32[512]{0:T(512)S(1)}, f32[512,768]{1,0:T(8,128)S(1)}) fusion(f32[512]{0:T(512)S(1)} %copy-done.52, f32[512]{0:T(512)S(1)} %copy-done.49, bf16[64,768]{1,0:T(8,128)(2,1)} %collective-permute-done.1, bf16[384,768]{1,0:T(8,128)(2,1)S(1)} %bitcast.206, ...), kind=kOutput, calls=%fused_computation.82 | convolution fusion | flops 1826879744 | bytes 8073728 | tf_op jit(solution)/shard_map/dot_general | solution.py:93
  226.3 2.9 fusion.87
  233.9 2.3 fusion.37
  236.6 2.2 collective-permute-start.18
  238.8 2.6 fusion.5
  250.4 8.1 %collective-permute-done.22 = bf16[2,96,1280]{2,1,0:T(8,128)(2,1)S(1)} collective-permute-done((bf16[2,96,1280]{2,1,0:T(8,128)(2,1)S(1)}, bf16[2,96,1280]{2,1,0:T(8,128)(2,1)S(1)}, u32[]{:S(2)}, u32[]{:S(2)}) %collective-permute-start.22) | collective-permute-done | bytes 491552 | tf_op jit(solution)/shard_map/ppermute | solution.py:23
  258.9 12.6 %collective-permute-done.23 = bf16[2,96,1280]{2,1,0:T(8,128)(2,1)S(1)} collective-permute-done((bf16[2,96,1280]{2,1,0:T(8,128)(2,1)S(1)}, bf16[2,96,1280]{2,1,0:T(8,128)(2,1)S(1)}, u32[]{:S(2)}, u32[]{:S(2)}) %collective-permute-start.23) | collective-permute-done | bytes 491552 | tf_op jit(solution)/shard_map/ppermute | solution.py:23
  275.6 6.5 %collective-permute-done.25 = bf16[96,1280]{1,0:T(8,128)(2,1)S(1)} collective-permute-done((bf16[96,1280]{1,0:T(8,128)(2,1)S(1)}, bf16[96,1280]{1,0:T(8,128)(2,1)S(1)}, u32[]{:S(2)}, u32[]{:S(2)}) %collective-permute-start.25) | collective-permute-done | bytes 245792 | tf_op jit(solution)/shard_map/ppermute | solution.py:23
  282.0 3.6 %collective-permute-start.19 = (bf16[64,768]{1,0:T(8,128)(2,1)S(1)}, bf16[64,768]{1,0:T(8,128)(2,1)S(1)}, u32[]{:S(2)}, u32[]{:S(2)}) collective-permute-start(bf16[64,768]{1,0:T(8,128)(2,1)S(1)} %get-tuple-element.102), channel_id=1, source_target_pairs={{0,1},{1,2},{2,3},{3,4},{4,5},{5,6},{6,7},{7,8},{8,9},{9,10},{10,1... | collective-permute-start | bytes 294920 | tf_op jit(solution)/shard_map/ppermute | solution.py:42
  286.7 19.4 %collective-permute-done.38 = bf16[2,528,384]{2,1,0:T(8,128)(2,1)S(1)} collective-permute-done((bf16[2,528,384]{2,1,0:T(8,128)(2,1)S(1)}, bf16[2,528,384]{2,1,0:T(8,128)(2,1)S(1)}, u32[]{:S(2)}, u32[]{:S(2)}) %collective-permute-start.38) | collective-permute-done | bytes 811040 | tf_op jit(solution)/shard_map/ppermute | solution.py:23
  306.1 2.7 collective-permute-start.28
  309.9 5.2 %collective-permute-done.27 = bf16[96,1280]{1,0:T(8,128)(2,1)S(1)} collective-permute-done((bf16[96,1280]{1,0:T(8,128)(2,1)S(1)}, bf16[96,1280]{1,0:T(8,128)(2,1)S(1)}, u32[]{:S(2)}, u32[]{:S(2)}) %collective-permute-start.27) | collective-permute-done | bytes 245792 | tf_op jit(solution)/shard_map/ppermute | solution.py:33
  315.3 6.6 %collective-permute-done.40 = bf16[528,384]{1,0:T(8,128)(2,1)S(1)} collective-permute-done((bf16[528,384]{1,0:T(8,128)(2,1)S(1)}, bf16[528,384]{1,0:T(8,128)(2,1)S(1)}, u32[]{:S(2)}, u32[]{:S(2)}) %collective-permute-start.40) | collective-permute-done | bytes 405536 | tf_op jit(solution)/shard_map/ppermute | solution.py:23
  322.7 2.3 collective-permute-start.43
  325.1 8.5 %collective-permute-done.41 = bf16[528,384]{1,0:T(8,128)(2,1)S(1)} collective-permute-done((bf16[528,384]{1,0:T(8,128)(2,1)S(1)}, bf16[528,384]{1,0:T(8,128)(2,1)S(1)}, u32[]{:S(2)}, u32[]{:S(2)}) %collective-permute-start.41) | collective-permute-done | bytes 405536 | tf_op jit(solution)/shard_map/ppermute | solution.py:33
  333.6 3.4 collective-permute-start.30
  337.0 6.2 %collective-permute-done.42 = bf16[528,384]{1,0:T(8,128)(2,1)S(1)} collective-permute-done((bf16[528,384]{1,0:T(8,128)(2,1)S(1)}, bf16[528,384]{1,0:T(8,128)(2,1)S(1)}, u32[]{:S(2)}, u32[]{:S(2)}) %collective-permute-start.42) | collective-permute-done | bytes 405536 | tf_op jit(solution)/shard_map/ppermute | solution.py:33
  344.6 9.1 %collective-permute-done.44 = bf16[528,384]{1,0:T(8,128)(2,1)S(1)} collective-permute-done((bf16[528,384]{1,0:T(8,128)(2,1)S(1)}, bf16[528,384]{1,0:T(8,128)(2,1)S(1)}, u32[]{:S(2)}, u32[]{:S(2)}) %collective-permute-start.44) | collective-permute-done | bytes 405536 | tf_op jit(solution)/shard_map/ppermute | solution.py:33
  (322 shorter events, 122.8 us)
Async XLA Ops:
  8.4 64.5 %collective-permute-start.10 = (bf16[264,768]{1,0:T(8,128)(2,1)}, bf16[264,768]{1,0:T(8,128)(2,1)}, u32[]{:S(2)}, u32[]{:S(2)}) collective-permute-start(bf16[264,768]{1,0:T(8,128)(2,1)} %dynamic-slice_dynamic-update-slice_fusion), channel_id=1, source_target_pairs={{0,16},{16,0},{32,48},{48,32},{64,80},{80,64},{96,112},{112,96},{1... | collective-permute-start | bytes 1216520 | tf_op jit(solution)/shard_map/ppermute | solution.py:23
  12.0 64.1 %collective-permute-start.11 = (bf16[264,768]{1,0:T(8,128)(2,1)}, bf16[264,768]{1,0:T(8,128)(2,1)}, u32[]{:S(2)}, u32[]{:S(2)}) collective-permute-start(bf16[264,768]{1,0:T(8,128)(2,1)} %dynamic-slice_dynamic-update-slice_fusion), channel_id=1, source_target_pairs={{0,96},{16,112},{32,0},{48,16},{64,32},{80,48},{96,64},{112,80},{1... | collective-permute-start | bytes 1216520 | tf_op jit(solution)/shard_map/ppermute | solution.py:23
  12.6 65.7 %collective-permute-start.13 = (bf16[264,768]{1,0:T(8,128)(2,1)}, bf16[264,768]{1,0:T(8,128)(2,1)}, u32[]{:S(2)}, u32[]{:S(2)}) collective-permute-start(bf16[264,768]{1,0:T(8,128)(2,1)} %dynamic-slice_dynamic-update-slice_fusion), channel_id=1, source_target_pairs={{0,64},{16,80},{32,96},{48,112},{64,0},{80,16},{96,32},{112,48},{1... | collective-permute-start | bytes 1216520 | tf_op jit(solution)/shard_map/ppermute | solution.py:23
  15.0 13.7 %collective-permute-start = (bf16[64,768]{1,0:T(8,128)(2,1)}, bf16[64,768]{1,0:T(8,128)(2,1)}, u32[]{:S(2)}, u32[]{:S(2)}) collective-permute-start(bf16[64,768]{1,0:T(8,128)(2,1)} %get-tuple-element.103), channel_id=1, source_target_pairs={{0,1},{1,2},{2,3},{3,4},{4,5},{5,6},{6,7},{7,8},{8,9},{9,10},{10,1... | collective-permute-start | bytes 294920 | tf_op jit(solution)/shard_map/ppermute | solution.py:42
  19.7 9.0 %collective-permute-start.1 = (bf16[64,768]{1,0:T(8,128)(2,1)}, bf16[64,768]{1,0:T(8,128)(2,1)}, u32[]{:S(2)}, u32[]{:S(2)}) collective-permute-start(bf16[64,768]{1,0:T(8,128)(2,1)} %get-tuple-element.104), channel_id=1, source_target_pairs={{1,0},{2,1},{3,2},{4,3},{5,4},{6,5},{7,6},{8,7},{9,8},{10,9},{11,1... | collective-permute-start | bytes 294920 | tf_op jit(solution)/shard_map/ppermute | solution.py:42
  28.7 7.8 %collective-permute-start.2 = (bf16[48,2432]{1,0:T(8,128)(2,1)}, bf16[48,2432]{1,0:T(8,128)(2,1)S(1)}, u32[]{:S(2)}, u32[]{:S(2)}) collective-permute-start(bf16[48,2432]{1,0:T(8,128)(2,1)} %pad_maximum_fusion.12), channel_id=1, source_target_pairs={{0,16},{16,0},{32,48},{48,32},{64,80},{80,64},{96,112},{112,96},{1... | collective-permute-start | bytes 700424 | tf_op jit(solution)/shard_map/ppermute | solution.py:23
  28.7 9.9 %collective-permute-start.3 = (bf16[48,2432]{1,0:T(8,128)(2,1)}, bf16[48,2432]{1,0:T(8,128)(2,1)S(1)}, u32[]{:S(2)}, u32[]{:S(2)}) collective-permute-start(bf16[48,2432]{1,0:T(8,128)(2,1)} %pad_maximum_fusion.12), channel_id=1, source_target_pairs={{0,96},{16,112},{32,0},{48,16},{64,32},{80,48},{96,64},{112,80},{1... | collective-permute-start | bytes 700424 | tf_op jit(solution)/shard_map/ppermute | solution.py:23
  31.8 74.8 %copy-start.48 = (f32[512]{0:T(512)}, f32[512]{0:T(512)S(1)}, u32[]{:S(2)}) copy-start(f32[512]{0:T(512)S(1)} %broadcast_multiply_fusion.5) | copy-start | bytes 6148
  36.5 9.0 %collective-permute-start.5 = (bf16[48,2432]{1,0:T(8,128)(2,1)S(1)}, bf16[48,2432]{1,0:T(8,128)(2,1)S(1)}, u32[]{:S(2)}, u32[]{:S(2)}) collective-permute-start(bf16[48,2432]{1,0:T(8,128)(2,1)S(1)} %copy-done.43), channel_id=1, source_target_pairs={{0,64},{16,80},{32,96},{48,112},{64,0},{80,16},{96,32},{112,48},{1... | collective-permute-start | bytes 700424 | tf_op jit(solution)/shard_map/ppermute | solution.py:23
  38.7 11.7 %collective-permute-start.4 = (bf16[48,2432]{1,0:T(8,128)(2,1)S(1)}, bf16[48,2432]{1,0:T(8,128)(2,1)S(1)}, u32[]{:S(2)}, u32[]{:S(2)}) collective-permute-start(bf16[48,2432]{1,0:T(8,128)(2,1)S(1)} %collective-permute-done.2), channel_id=1, source_target_pairs={{0,96},{16,112},{32,0},{48,16},{64,32},{80,48},{96,64},{112,80},{1... | collective-permute-start | bytes 700424 | tf_op jit(solution)/shard_map/ppermute | solution.py:23
  45.4 52.6 %collective-permute-start.15 = (bf16[264,768]{1,0:T(8,128)(2,1)}, bf16[264,768]{1,0:T(8,128)(2,1)S(1)}, u32[]{:S(2)}, u32[]{:S(2)}) collective-permute-start(bf16[264,768]{1,0:T(8,128)(2,1)} %dynamic-slice_dynamic-update-slice_fusion), channel_id=1, source_target_pairs={{0,32},{16,48},{32,64},{48,80},{64,96},{80,112},{96,0},{112,16},{1... | collective-permute-start | bytes 1216520 | tf_op jit(solution)/shard_map/ppermute | solution.py:23
  50.4 8.3 %collective-permute-start.6 = (bf16[48,2432]{1,0:T(8,128)(2,1)S(1)}, bf16[48,2432]{1,0:T(8,128)(2,1)S(1)}, u32[]{:S(2)}, u32[]{:S(2)}) collective-permute-start(bf16[48,2432]{1,0:T(8,128)(2,1)S(1)} %collective-permute-done.5), channel_id=1, source_target_pairs={{0,16},{16,0},{32,48},{48,32},{64,80},{80,64},{96,112},{112,96},{1... | collective-permute-start | bytes 700424 | tf_op jit(solution)/shard_map/ppermute | solution.py:23
  58.7 5.9 %collective-permute-start.7 = (bf16[48,2432]{1,0:T(8,128)(2,1)S(1)}, bf16[48,2432]{1,0:T(8,128)(2,1)S(1)}, u32[]{:S(2)}, u32[]{:S(2)}) collective-permute-start(bf16[48,2432]{1,0:T(8,128)(2,1)S(1)} %copy-done.43), channel_id=1, source_target_pairs={{0,32},{16,48},{32,64},{48,80},{64,96},{80,112},{96,0},{112,16},{1... | collective-permute-start | bytes 700424 | tf_op jit(solution)/shard_map/ppermute | solution.py:23
  64.6 4.9 %collective-permute-start.8 = (bf16[48,2432]{1,0:T(8,128)(2,1)S(1)}, bf16[48,2432]{1,0:T(8,128)(2,1)S(1)}, u32[]{:S(2)}, u32[]{:S(2)}) collective-permute-start(bf16[48,2432]{1,0:T(8,128)(2,1)S(1)} %collective-permute-done.2), channel_id=1, source_target_pairs={{0,32},{16,48},{32,64},{48,80},{64,96},{80,112},{96,0},{112,16},{1... | collective-permute-start | bytes 700424 | tf_op jit(solution)/shard_map/ppermute | solution.py:23
  69.5 32.0 %collective-permute-start.9 = (bf16[8,48,2432]{2,1,0:T(8,128)(2,1)S(1)}, bf16[8,48,2432]{2,1,0:T(8,128)(2,1)S(1)}, u32[]{:S(2)}, u32[]{:S(2)}) collective-permute-start(bf16[8,48,2432]{2,1,0:T(8,128)(2,1)S(1)} %bitcast_dynamic-update-slice_fusion.10), channel_id=1, source_target_pairs={{0,1},{1,0},{2,3},{3,2},{4,5},{5,4},{6,7},{7,6},{8,9},{9,8},{10,11... | collective-permute-start | bytes 5603336 | tf_op jit(solution)/shard_map/ppermute | solution.py:33
  73.0 33.6 %copy-start.51 = (f32[512]{0:T(512)}, f32[512]{0:T(512)S(1)}, u32[]{:S(2)}) copy-start(f32[512]{0:T(512)S(1)} %add_rsqrt_fusion.1) | copy-start | bytes 6148
  73.0 12.5 %collective-permute-start.12 = (bf16[264,768]{1,0:T(8,128)(2,1)}, bf16[264,768]{1,0:T(8,128)(2,1)S(1)}, u32[]{:S(2)}, u32[]{:S(2)}) collective-permute-start(bf16[264,768]{1,0:T(8,128)(2,1)} %collective-permute-done.10), channel_id=1, source_target_pairs={{0,96},{16,112},{32,0},{48,16},{64,32},{80,48},{96,64},{112,80},{1... | collective-permute-start | bytes 1216520 | tf_op jit(solution)/shard_map/ppermute | solution.py:23
  76.1 165.6 %collective-permute-start.36 = (bf16[384,384]{1,0:T(8,128)(2,1)}, bf16[384,384]{1,0:T(8,128)(2,1)}, u32[]{:S(2)}, u32[]{:S(2)}) collective-permute-start(bf16[384,384]{1,0:T(8,128)(2,1)} %dynamic-slice_bitcast_fusion.3), channel_id=1, source_target_pairs={{0,1},{1,0},{2,3},{3,2},{4,5},{5,4},{6,7},{7,6},{8,9},{9,8},{10,11... | collective-permute-start | bytes 884744 | tf_op jit(solution)/shard_map/ppermute | solution.py:33
  78.2 20.6 %collective-permute-start.16 = (bf16[264,768]{1,0:T(8,128)(2,1)}, bf16[264,768]{1,0:T(8,128)(2,1)S(1)}, u32[]{:S(2)}, u32[]{:S(2)}) collective-permute-start(bf16[264,768]{1,0:T(8,128)(2,1)} %collective-permute-done.10), channel_id=1, source_target_pairs={{0,32},{16,48},{32,64},{48,80},{64,96},{80,112},{96,0},{112,16},{1... | collective-permute-start | bytes 1216520 | tf_op jit(solution)/shard_map/ppermute | solution.py:23
  85.4 11.8 %collective-permute-start.14 = (bf16[264,768]{1,0:T(8,128)(2,1)}, bf16[264,768]{1,0:T(8,128)(2,1)S(1)}, u32[]{:S(2)}, u32[]{:S(2)}) collective-permute-start(bf16[264,768]{1,0:T(8,128)(2,1)} %collective-permute-done.13), channel_id=1, source_target_pairs={{0,16},{16,0},{32,48},{48,32},{64,80},{80,64},{96,112},{112,96},{1... | collective-permute-start | bytes 1216520 | tf_op jit(solution)/shard_map/ppermute | solution.py:23
  99.6 34.9 %collective-permute-start.17 = (bf16[8,264,768]{2,1,0:T(8,128)(2,1)}, bf16[8,264,768]{2,1,0:T(8,128)(2,1)}, u32[]{:S(2)}, u32[]{:S(2)}) collective-permute-start(bf16[8,264,768]{2,1,0:T(8,128)(2,1)} %bitcast_dynamic-update-slice_fusion), channel_id=1, source_target_pairs={{0,1},{1,0},{2,3},{3,2},{4,5},{5,4},{6,7},{7,6},{8,9},{9,8},{10,11... | collective-permute-start | bytes 9732104 | tf_op jit(solution)/shard_map/ppermute | solution.py:33
  134.1 99.2 %collective-permute-start.31 = (bf16[384,768]{0,1:T(8,128)(2,1)}, bf16[384,768]{0,1:T(8,128)(2,1)}, u32[]{:S(2)}, u32[]{:S(2)}) collective-permute-start(bf16[384,768]{0,1:T(8,128)(2,1)} %bitcast.222), channel_id=1, source_target_pairs={{0,1},{1,0},{2,3},{3,2},{4,5},{5,4},{6,7},{7,6},{8,9},{9,8},{10,11... | collective-permute-start | bytes 1769480 | tf_op jit(solution)/shard_map/ppermute | solution.py:33
  158.6 77.6 %collective-permute-start.33 = (bf16[384,768]{1,0:T(8,128)(2,1)}, bf16[384,768]{1,0:T(8,128)(2,1)}, u32[]{:S(2)}, u32[]{:S(2)}) collective-permute-start(bf16[384,768]{1,0:T(8,128)(2,1)} %multiply_convert_fusion.3), channel_id=1, source_target_pairs={{0,1},{1,0},{2,3},{3,2},{4,5},{5,4},{6,7},{7,6},{8,9},{9,8},{10,11... | collective-permute-start | bytes 1769480 | tf_op jit(solution)/shard_map/ppermute | solution.py:33
  221.3 15.3 %collective-permute-start.34 = (bf16[384,1152]{1,0:T(8,128)(2,1)}, bf16[384,1152]{1,0:T(8,128)(2,1)}, u32[]{:S(2)}, u32[]{:S(2)}) collective-permute-start(bf16[384,1152]{1,0:T(8,128)(2,1)} %fusion.51), channel_id=1, source_target_pairs={{0,1},{1,0},{2,3},{3,2},{4,5},{5,4},{6,7},{7,6},{8,9},{9,8},{10,11... | collective-permute-start | bytes 2654216 | tf_op jit(solution)/shard_map/ppermute | solution.py:33
  230.0 3.6 collective-permute-start.32
  233.3 8.5 %collective-permute-start.35 = (bf16[384,1152]{1,0:T(8,128)(2,1)}, bf16[384,1152]{1,0:T(8,128)(2,1)S(1)}, u32[]{:S(2)}, u32[]{:S(2)}) collective-permute-start(bf16[384,1152]{1,0:T(8,128)(2,1)} %get-tuple-element.75), channel_id=1, source_target_pairs={{0,1},{1,0},{2,3},{3,2},{4,5},{5,4},{6,7},{7,6},{8,9},{9,8},{10,11... | collective-permute-start | bytes 2654216 | tf_op jit(solution)/shard_map/ppermute | solution.py:33
  233.5 10.1 %collective-permute-start.21 = (bf16[512,1152]{0,1:T(8,128)(2,1)}, bf16[512,1152]{0,1:T(8,128)(2,1)S(1)}, u32[]{:S(2)}, u32[]{:S(2)}) collective-permute-start(bf16[512,1152]{0,1:T(8,128)(2,1)} %constant_dynamic-slice_fusion.1), channel_id=1, source_target_pairs={{0,1},{1,0},{2,3},{3,2},{4,5},{5,4},{6,7},{7,6},{8,9},{9,8},{10,11... | collective-permute-start | bytes 3538952 | tf_op jit(solution)/shard_map/ppermute | solution.py:33
  236.3 7.3 %collective-permute-start.20 = (bf16[512,768]{1,0:T(8,128)(2,1)S(1)}, bf16[512,768]{1,0:T(8,128)(2,1)S(1)}, u32[]{:S(2)}, u32[]{:S(2)}) collective-permute-start(bf16[512,768]{1,0:T(8,128)(2,1)S(1)} %copy-done.28), channel_id=1, source_target_pairs={{0,1},{1,0},{2,3},{3,2},{4,5},{5,4},{6,7},{7,6},{8,9},{9,8},{10,11... | collective-permute-start | bytes 2359304 | tf_op jit(solution)/shard_map/ppermute | solution.py:33
  236.6 107.0 %collective-permute-start.18 = (bf16[64,768]{1,0:T(8,128)(2,1)S(1)}, bf16[64,768]{1,0:T(8,128)(2,1)S(1)}, u32[]{:S(2)}, u32[]{:S(2)}) collective-permute-start(bf16[64,768]{1,0:T(8,128)(2,1)S(1)} %get-tuple-element.101), channel_id=1, source_target_pairs={{1,0},{2,1},{3,2},{4,3},{5,4},{6,5},{7,6},{8,7},{9,8},{10,9},{11,1... | collective-permute-start | bytes 294920 | tf_op jit(solution)/shard_map/ppermute | solution.py:42
  245.2 13.3 %collective-permute-start.22 = (bf16[2,96,1280]{2,1,0:T(8,128)(2,1)S(1)}, bf16[2,96,1280]{2,1,0:T(8,128)(2,1)S(1)}, u32[]{:S(2)}, u32[]{:S(2)}) collective-permute-start(bf16[2,96,1280]{2,1,0:T(8,128)(2,1)S(1)} %get-tuple-element.85), channel_id=1, source_target_pairs={{0,32},{16,48},{32,64},{48,80},{64,96},{80,112},{96,0},{112,16},{1... | collective-permute-start | bytes 1474568 | tf_op jit(solution)/shard_map/ppermute | solution.py:23
  246.6 24.9 %collective-permute-start.23 = (bf16[2,96,1280]{2,1,0:T(8,128)(2,1)S(1)}, bf16[2,96,1280]{2,1,0:T(8,128)(2,1)S(1)}, u32[]{:S(2)}, u32[]{:S(2)}) collective-permute-start(bf16[2,96,1280]{2,1,0:T(8,128)(2,1)S(1)} %get-tuple-element.86), channel_id=1, source_target_pairs={{0,96},{16,112},{32,0},{48,16},{64,32},{80,48},{96,64},{112,80},{1... | collective-permute-start | bytes 1474568 | tf_op jit(solution)/shard_map/ppermute | solution.py:23
  246.7 26.2 %collective-permute-start.24 = (bf16[2,96,1280]{2,1,0:T(8,128)(2,1)S(1)}, bf16[2,96,1280]{2,1,0:T(8,128)(2,1)S(1)}, u32[]{:S(2)}, u32[]{:S(2)}) collective-permute-start(bf16[2,96,1280]{2,1,0:T(8,128)(2,1)S(1)} %get-tuple-element.87), channel_id=1, source_target_pairs={{0,64},{16,80},{32,96},{48,112},{64,0},{80,16},{96,32},{112,48},{1... | collective-permute-start | bytes 1474568 | tf_op jit(solution)/shard_map/ppermute | solution.py:23
  248.6 37.8 %collective-permute-start.37 = (bf16[2,528,384]{2,1,0:T(8,128)(2,1)S(1)}, bf16[2,528,384]{2,1,0:T(8,128)(2,1)S(1)}, u32[]{:S(2)}, u32[]{:S(2)}) collective-permute-start(bf16[2,528,384]{2,1,0:T(8,128)(2,1)S(1)} %get-tuple-element.80), channel_id=1, source_target_pairs={{0,32},{16,48},{32,64},{48,80},{64,96},{80,112},{96,0},{112,16},{1... | collective-permute-start | bytes 2433032 | tf_op jit(solution)/shard_map/ppermute | solution.py:23
  258.5 47.6 %collective-permute-start.38 = (bf16[2,528,384]{2,1,0:T(8,128)(2,1)S(1)}, bf16[2,528,384]{2,1,0:T(8,128)(2,1)S(1)}, u32[]{:S(2)}, u32[]{:S(2)}) collective-permute-start(bf16[2,528,384]{2,1,0:T(8,128)(2,1)S(1)} %get-tuple-element.82), channel_id=1, source_target_pairs={{0,96},{16,112},{32,0},{48,16},{64,32},{80,48},{96,64},{112,80},{1... | collective-permute-start | bytes 2433032 | tf_op jit(solution)/shard_map/ppermute | solution.py:23
  271.5 34.6 %collective-permute-start.39 = (bf16[2,528,384]{2,1,0:T(8,128)(2,1)S(1)}, bf16[2,528,384]{2,1,0:T(8,128)(2,1)S(1)}, u32[]{:S(2)}, u32[]{:S(2)}) collective-permute-start(bf16[2,528,384]{2,1,0:T(8,128)(2,1)S(1)} %get-tuple-element.81), channel_id=1, source_target_pairs={{0,64},{16,80},{32,96},{48,112},{64,0},{80,16},{96,32},{112,48},{1... | collective-permute-start | bytes 2433032 | tf_op jit(solution)/shard_map/ppermute | solution.py:23
  273.2 8.9 %collective-permute-start.25 = (bf16[96,1280]{1,0:T(8,128)(2,1)S(1)}, bf16[96,1280]{1,0:T(8,128)(2,1)S(1)}, u32[]{:S(2)}, u32[]{:S(2)}) collective-permute-start(bf16[96,1280]{1,0:T(8,128)(2,1)S(1)} %select_bitcast_fusion.1), channel_id=1, source_target_pairs={{0,16},{16,0},{32,48},{48,32},{64,80},{80,64},{96,112},{112,96},{1... | collective-permute-start | bytes 737288 | tf_op jit(solution)/shard_map/ppermute | solution.py:23
  282.0 61.5 %collective-permute-start.19 = (bf16[64,768]{1,0:T(8,128)(2,1)S(1)}, bf16[64,768]{1,0:T(8,128)(2,1)S(1)}, u32[]{:S(2)}, u32[]{:S(2)}) collective-permute-start(bf16[64,768]{1,0:T(8,128)(2,1)S(1)} %get-tuple-element.102), channel_id=1, source_target_pairs={{0,1},{1,2},{2,3},{3,4},{4,5},{5,6},{6,7},{7,8},{8,9},{9,10},{10,1... | collective-permute-start | bytes 294920 | tf_op jit(solution)/shard_map/ppermute | solution.py:42
  286.4 22.8 %collective-permute-start.26 = (bf16[96,1280]{1,0:T(8,128)(2,1)S(1)}, bf16[96,1280]{1,0:T(8,128)(2,1)S(1)}, u32[]{:S(2)}, u32[]{:S(2)}) collective-permute-start(bf16[96,1280]{1,0:T(8,128)(2,1)S(1)} %fusion.64), channel_id=1, source_target_pairs={{0,4},{1,5},{2,6},{3,7},{4,0},{5,1},{6,2},{7,3},{8,12},{9,13},{10,... | collective-permute-start | bytes 737288 | tf_op jit(solution)/shard_map/ppermute | solution.py:33
  306.1 9.0 %collective-permute-start.27 = (bf16[96,1280]{1,0:T(8,128)(2,1)S(1)}, bf16[96,1280]{1,0:T(8,128)(2,1)S(1)}, u32[]{:S(2)}, u32[]{:S(2)}) collective-permute-start(bf16[96,1280]{1,0:T(8,128)(2,1)S(1)} %fusion.64), channel_id=1, source_target_pairs={{0,2},{1,3},{2,4},{3,5},{4,6},{5,7},{6,0},{7,1},{8,10},{9,11},{10,... | collective-permute-start | bytes 737288 | tf_op jit(solution)/shard_map/ppermute | solution.py:33
  306.1 9.0 %collective-permute-start.28 = (bf16[96,1280]{1,0:T(8,128)(2,1)S(1)}, bf16[96,1280]{1,0:T(8,128)(2,1)S(1)}, u32[]{:S(2)}, u32[]{:S(2)}) collective-permute-start(bf16[96,1280]{1,0:T(8,128)(2,1)S(1)} %fusion.64), channel_id=1, source_target_pairs={{0,6},{1,7},{2,0},{3,1},{4,2},{5,3},{6,4},{7,5},{8,14},{9,15},{10,... | collective-permute-start | bytes 737288 | tf_op jit(solution)/shard_map/ppermute | solution.py:33
  309.2 12.7 %collective-permute-start.40 = (bf16[528,384]{1,0:T(8,128)(2,1)S(1)}, bf16[528,384]{1,0:T(8,128)(2,1)S(1)}, u32[]{:S(2)}, u32[]{:S(2)}) collective-permute-start(bf16[528,384]{1,0:T(8,128)(2,1)S(1)} %select_bitcast_fusion), channel_id=1, source_target_pairs={{0,16},{16,0},{32,48},{48,32},{64,80},{80,64},{96,112},{112,96},{1... | collective-permute-start | bytes 1216520 | tf_op jit(solution)/shard_map/ppermute | solution.py:23
  315.2 7.5 %collective-permute-start.29 = (bf16[96,1280]{1,0:T(8,128)(2,1)S(1)}, bf16[96,1280]{1,0:T(8,128)(2,1)S(1)}, u32[]{:S(2)}, u32[]{:S(2)}) collective-permute-start(bf16[96,1280]{1,0:T(8,128)(2,1)S(1)} %add_convert_fusion.8), channel_id=1, source_target_pairs={{0,8},{1,9},{2,10},{3,11},{4,12},{5,13},{6,14},{7,15},{8,0},{9,1},... | collective-permute-start | bytes 737288 | tf_op jit(solution)/shard_map/ppermute | solution.py:33
  322.1 11.5 %collective-permute-start.41 = (bf16[528,384]{1,0:T(8,128)(2,1)S(1)}, bf16[528,384]{1,0:T(8,128)(2,1)S(1)}, u32[]{:S(2)}, u32[]{:S(2)}) collective-permute-start(bf16[528,384]{1,0:T(8,128)(2,1)S(1)} %fusion.53), channel_id=1, source_target_pairs={{0,4},{1,5},{2,6},{3,7},{4,0},{5,1},{6,2},{7,3},{8,12},{9,13},{10,... | collective-permute-start | bytes 1216520 | tf_op jit(solution)/shard_map/ppermute | solution.py:33
  322.2 21.1 %collective-permute-start.42 = (bf16[528,384]{1,0:T(8,128)(2,1)S(1)}, bf16[528,384]{1,0:T(8,128)(2,1)S(1)}, u32[]{:S(2)}, u32[]{:S(2)}) collective-permute-start(bf16[528,384]{1,0:T(8,128)(2,1)S(1)} %fusion.53), channel_id=1, source_target_pairs={{0,2},{1,3},{2,4},{3,5},{4,6},{5,7},{6,0},{7,1},{8,10},{9,11},{10,... | collective-permute-start | bytes 1216520 | tf_op jit(solution)/shard_map/ppermute | solution.py:33
  322.7 20.6 %collective-permute-start.43 = (bf16[528,384]{1,0:T(8,128)(2,1)S(1)}, bf16[528,384]{1,0:T(8,128)(2,1)S(1)}, u32[]{:S(2)}, u32[]{:S(2)}) collective-permute-start(bf16[528,384]{1,0:T(8,128)(2,1)S(1)} %fusion.53), channel_id=1, source_target_pairs={{0,6},{1,7},{2,0},{3,1},{4,2},{5,3},{6,4},{7,5},{8,14},{9,15},{10,... | collective-permute-start | bytes 1216520 | tf_op jit(solution)/shard_map/ppermute | solution.py:33
  333.6 11.0 %collective-permute-start.30 = (bf16[96,1280]{1,0:T(8,128)(2,1)S(1)}, bf16[96,1280]{1,0:T(8,128)(2,1)S(1)}, u32[]{:S(2)}, u32[]{:S(2)}) collective-permute-start(bf16[96,1280]{1,0:T(8,128)(2,1)S(1)} %add_convert_fusion.7), channel_id=1, source_target_pairs={{0,1},{1,0},{2,3},{3,2},{4,5},{5,4},{6,7},{7,6},{8,9},{9,8},{10,11... | collective-permute-start | bytes 737288 | tf_op jit(solution)/shard_map/ppermute | solution.py:33
  343.5 10.3 %collective-permute-start.44 = (bf16[528,384]{1,0:T(8,128)(2,1)S(1)}, bf16[528,384]{1,0:T(8,128)(2,1)S(1)}, u32[]{:S(2)}, u32[]{:S(2)}) collective-permute-start(bf16[528,384]{1,0:T(8,128)(2,1)S(1)} %add_convert_fusion.2), channel_id=1, source_target_pairs={{0,8},{1,9},{2,10},{3,11},{4,12},{5,13},{6,14},{7,15},{8,0},{9,1},... | collective-permute-start | bytes 1216520 | tf_op jit(solution)/shard_map/ppermute | solution.py:33
  353.9 3.2 collective-permute-start.45
  (57 other events, 296.8 us)
